TPU v7x, 512 devices: a whole 4x8x8 slice. The times are simulated.
512 devices in a mesh: loop: 32 (over x_hi, y, core), orb: 16 (over z, x_lo).
Axes of the slice: x: 4 (x_hi: 2, x_lo: 2; x = x_hi * 2 + x_lo), y: 8, z: 8, core: 2. Of those that a mesh axis runs over, the one named last changes fastest.
Arguments:
- cholesky: bfloat16 [4096, 65536], P('loop', 'orb'), may hold values from -0.0234375 to 0.0234375
- green_half: bfloat16 [1536, 65536], P('loop', 'orb'), may hold values from -6 to 6
- partners: int32 [256, 2], replicated, may hold values from 0 to 1535, as said below
Outputs:
- green_copied: bfloat16 [1536, 65536], P('loop', 'orb')
- force_bias: float32 [1536, 4096], P('orb', 'loop')
Inputs may be any that keep to these rules, and one draw needn't show every extreme that they name: `partners`: column 0 is a source walker, column 1 a destination walker. Destinations are distinct, sources are distinct, and no source is a destination. Each block of 48 consecutive walkers holds exactly 8 destinations and exactly 8 sources.
All inputs are finite; a program needn't handle non-finite values.
Results may differ from a plain program's by a relative error of at most 0.001.
Values may be sent and summed in bfloat16 or wider, within the bound.
A program may use at most 64 MiB of HBM per device.

v0:
```python
import jax
import jax.numpy as jnp
from jax import lax
from jax.sharding import PartitionSpec as P


def contract(shard_rows, cholesky):
    return lax.dot_general(
        shard_rows, cholesky, (((1,), (1,)), ((), ())), preferred_element_type=jnp.float32
    )


def local(cholesky, green_half, partners):
    loop_count = lax.axis_size("loop")
    block_rows = green_half.shape[0]
    walkers = block_rows * loop_count
    events = partners.shape[0]
    per_block = events // loop_count
    sources = partners[:, 0]
    targets = partners[:, 1]
    first_row = lax.axis_index("loop") * block_rows
    walker_index = jnp.arange(walkers, dtype=jnp.int32)
    event_index = jnp.arange(events, dtype=jnp.int32)
    target_hits = targets[None, :] == walker_index[:, None]
    overwritten = jnp.any(target_hits, axis=1)
    anchor = jnp.where(
        overwritten, jnp.sum(jnp.where(target_hits, sources[None, :], 0), axis=1), walker_index
    )
    local_flags = lax.dynamic_slice_in_dim(overwritten, first_row, block_rows)
    local_targets = jnp.nonzero(local_flags, size=per_block)[0].astype(jnp.int32)
    compact_rows = walker_index.shape[0]
    vector_count = cholesky.shape[0]
    initial = (
        jnp.zeros((compact_rows, vector_count), jnp.float32),
        jnp.zeros((per_block, green_half.shape[1]), jnp.float32),
    )
    partial_value = contract(lax.all_gather(green_half, "loop", axis=0, tiled=True), cholesky)
    compact_bias = partial_value
    picked = initial[1]
    compact_bias, picked = (compact_bias, picked)
    owner_block = sources // block_rows
    earlier = event_index[None, :] < event_index[:, None]
    slot_rank = jnp.sum(
        jnp.logical_and(earlier, owner_block[None, :] == owner_block[:, None]).astype(jnp.int32),
        axis=1,
    )
    own_events = jnp.nonzero(owner_block == lax.axis_index("loop"), size=per_block)[0].astype(
        jnp.int32
    )
    packed = jnp.take(green_half, jnp.take(sources, own_events) - first_row, axis=0)
    arrived = lax.all_gather(packed, "loop", axis=0, tiled=True)
    event_of = jnp.sum(jnp.where(target_hits, event_index[None, :], 0), axis=1)
    local_events = jnp.take(event_of, first_row + local_targets)
    copied = jnp.take(arrived, jnp.take(owner_block * per_block + slot_rank, local_events), axis=0)
    new_green = green_half.at[local_targets].set(copied)
    full_bias = jnp.take(compact_bias, jnp.take(walker_index, anchor), axis=0)
    bias_share = lax.psum_scatter(full_bias, "orb", scatter_dimension=0, tiled=True)
    return (new_green, bias_share)


def solution(mesh):
    return jax.shard_map(
        local,
        mesh=mesh,
        in_specs=(P("loop", "orb"), P("loop", "orb"), P()),
        out_specs=(P("loop", "orb"), P("orb", "loop")),
        check_vma=False,
    )
```

profile of v0, /device:TPU:8, one launch (start us, length us, event | category | flops | bytes accessed | tf_op | source)
XLA Modules:
  0.0 306.2 jit_solution(8178744544804263753)
XLA Ops:
  7.2 1.8 copy.10
  9.2 0.7 fusion.20
  9.9 0.8 add_select_fusion
  10.6 0.3 reduce-window.27
  11.1 0.1 slice_reduce_fusion
  11.3 2.3 scatter_custom_fusion.1
  13.6 0.2 reduce-window.29
  13.8 0.6 fusion.8
  14.4 0.7 compare_select_fusion.6
  15.1 0.6 gather_fusion.5
  15.7 0.7 compare_and_fusion.2
  16.4 1.7 gather_fusion.1
  18.1 0.7 broadcast_select_fusion.1
  18.9 0.3 fusion
  19.2 0.8 fusion.17
  20.2 0.1 fusion.6
  20.3 0.9 scatter_custom_fusion
  21.2 0.2 select_n.234
  21.4 0.6 select_reduce_fusion
  22.0 8.4 %gather_fusion.2 = s32[1536]{0:T(1024)S(1)} fusion(s32[1536]{0:T(1024)S(1)} %iota.34, s32[2048]{0:T(1024)S(1)} %pad_clamp_fusion.1), kind=kCustom, calls=%fused_computation.5 | custom fusion | bytes 18432 | tf_op jit(solution)/shard_map/jit(_take)/gather | solution.py:56
  30.5 108.3 %all-gather.5.cloned.1.call-done = bf16[1536,4096]{1,0:T(8,128)(2,1)} async-done(((bf16[48,4096]{1,0:T(8,128)(2,1)}), bf16[1536,4096]{1,0:T(8,128)(2,1)}) %all-gather.5.cloned.1.call-update) | async-done | bytes 12582928 | tf_op jit(solution)/shard_map/all_gather | solution.py:37
  138.8 6.4 %fusion.21 = f32[1536,128]{1,0:T(8,128)S(1)} fusion(bf16[1536,4096]{1,0:T(8,128)(2,1)} %all-gather.5.cloned.1.call-done, bf16[128,4096]{1,0:T(8,128)(2,1)S(1)} %copy-done), kind=kOutput, calls=%fused_computation.85 | convolution fusion | flops 1610612736 | bytes 14417920 | tf_op jit(solution)/shard_map/dot_general | solution.py:8
  145.2 2.6 gather_fusion.3
  147.8 1.1 broadcast_select_fusion
  149.0 0.7 fusion.11
  149.7 0.6 gather_fusion
  150.4 0.7 compare_select_fusion.7
  151.1 0.2 convert_reduce_fusion
  151.3 0.6 gather_fusion.4
  152.0 72.4 %all-gather.3.cloned.1.call-done = bf16[256,4096]{1,0:T(8,128)(2,1)} async-done(((bf16[8,4096]{1,0:T(8,128)(2,1)}), bf16[256,4096]{1,0:T(8,128)(2,1)}) %all-gather.3.cloned.1.call-update) | async-done | bytes 2097168 | tf_op jit(solution)/shard_map/all_gather | solution.py:51
  224.4 1.9 scatter_custom_fusion.2
  226.4 73.3 %reduce-scatter.2.cloned.1.call-done = f32[96,128]{1,0:T(8,128)} async-done(((f32[1536,128]{1,0:T(8,128)}), f32[96,128]{1,0:T(8,128)}) %reduce-scatter.2.cloned.1.call-update) | async-done | bytes 49168 | tf_op jit(solution)/shard_map/reduce_scatter | solution.py:57
  (36 shorter events, 0.8 us)
Async XLA Ops:
  7.2 131.6 %copy-start = (bf16[128,4096]{1,0:T(8,128)(2,1)S(1)}, bf16[128,4096]{1,0:T(8,128)(2,1)}, u32[]{:S(2)}) copy-start(bf16[128,4096]{1,0:T(8,128)(2,1)} %param.5) | copy-start | bytes 3145732
  7.2 131.6 %all-gather.5.cloned.1.call-start = ((), (), s32[]{:S(2)}) async-start(), calls=%async_computation.2 | async-start | bytes 12976128 | tf_op jit(solution)/shard_map/all_gather | solution.py:37
  9.1 215.3 %all-gather.3.cloned.1.call-start = ((), (), s32[]{:S(2)}) async-start(), calls=%async_computation.1 | async-start | bytes 2162688 | tf_op jit(solution)/shard_map/all_gather | solution.py:51
  18.8 280.8 %reduce-scatter.2.cloned.1.call-start = ((), (), s32[]{:S(2)}) async-start(), calls=%async_computation.3 | async-start | bytes 835584 | tf_op jit(solution)/shard_map/reduce_scatter | solution.py:57
  147.8 76.6 %copy-start.1 = (bf16[48,4096]{1,0:T(8,128)(2,1)S(1)}, bf16[48,4096]{1,0:T(8,128)(2,1)}, u32[]{:S(2)}) copy-start(bf16[48,4096]{1,0:T(8,128)(2,1)} %copy.10) | copy-start | bytes 1179652
  226.3 73.3 %copy-start.2 = (bf16[48,4096]{1,0:T(8,128)(2,1)}, bf16[48,4096]{1,0:T(8,128)(2,1)S(1)}, u32[]{:S(2)}) copy-start(bf16[48,4096]{1,0:T(8,128)(2,1)S(1)} %scatter_custom_fusion.2) | copy-start | bytes 1179652
Sparse Core Ops, SparseCore 0:
  11.9 126.8 all-gather.4
  142.2 82.1 all-gather.2
  227.8 71.8 reduce-scatter.1
where the time goes:
time: 306 us
  waiting for transfers between devices  254 us (83%)
  local copies, waits for them, and re-layouts  16.8 us (5%)
  other arithmetic  14.9 us (5%)
  between operations  14 us (5%)
  matrix products  6.41 us (2%)
    all_gather x1, waiting for transfers between devices, local(): lax.all_gather(green_half, 'loop', axis=0, tiled=True)  108 us
    reduce_scatter x1, waiting for transfers between devices, local(): lax.psum_scatter(full_bias, 'orb', scatter_dimension=0, tiled=True)  73.3 us
    all_gather x1, waiting for transfers between devices, local(): arrived = lax.all_gather(packed, 'loop', axis=0, tiled=True)  72.4 us
    gather x2, local copies, waits for them, and re-layouts, local(): full_bias = jnp.take(compact_bias, jnp.take(walker_index, anchor), axis=0)  11 us
    dot_general x1, matrix products, contract(): lax.dot_general(shard_rows, cholesky, (((1,), (1,)), ((), ())), preferred...  6.41 us
  transfers between devices with their start and end apart: 3, of which 3 were waited for; matrix products, arithmetic and copies ran while one was open for 12% of the time, Pallas kernels for 0%

commit v1 on v0

--- a/solution.py
+++ b/solution.py
@@ -34,7 +34,12 @@
         jnp.zeros((compact_rows, vector_count), jnp.float32),
         jnp.zeros((per_block, green_half.shape[1]), jnp.float32),
     )
-    partial_value = contract(lax.all_gather(green_half, "loop", axis=0, tiled=True), cholesky)
+    partial_value = contract(
+        jnp.concatenate(
+            lax.all_to_all(jnp.stack([green_half] * lax.axis_size("loop")), "loop", 0, 0), axis=0
+        ),
+        cholesky,
+    )
     compact_bias = partial_value
     picked = initial[1]
     compact_bias, picked = (compact_bias, picked)

time: 306 us -> 407 us (1.33)
  waiting for transfers between devices: 254 us -> 340 us
  starting transfers between devices: 0.12 us -> 10.7 us
  local copies, waits for them, and re-layouts: 16.8 us -> 21 us
    all_to_all x0 -> x1, waiting for transfers between devices: none -> 262 us  [local(): lax.all_to_all(jnp.stack([green_half] * lax.axis_size('loop')), 'loop', 0...]
    all_gather x1 -> x0, waiting for transfers between devices: 108 us -> none  [local(): lax.all_gather(green_half, 'loop', axis=0, tiled=True)]
    all_gather x1, waiting for transfers between devices: 72.4 us -> 0.02 us  [local(): arrived = lax.all_gather(packed, 'loop', axis=0, tiled=True)]
    all_to_all x0 -> x1, starting transfers between devices: none -> 10.6 us  [local(): lax.all_to_all(jnp.stack([green_half] * lax.axis_size('loop')), 'loop', 0...]
    another operation x1 -> x2, local copies, waits for them, and re-layouts: 0.12 us -> 6.18 us  [the longest x1 6.06 us: local(): jnp.stack([green_half] * lax.axis_size('loop'))]
  transfers between devices with their start and end apart: 3 -> 3, of which waited for: 3 -> 2; matrix products, arithmetic and copies ran while one was open for 12% -> 8% of each run, Pallas kernels for 0% -> 0%
where the time goes in v1:
time: 407 us; the launch traced here: 406 us
  waiting for transfers between devices  340 us (84%)
  local copies, waits for them, and re-layouts  21 us (5%)
  between operations  15.7 us (4%)
  other arithmetic  13.1 us (3%)
  starting transfers between devices  10.7 us (3%)
  matrix products  6.41 us (2%)
    all_to_all x1, waiting for transfers between devices, local(): lax.all_to_all(jnp.stack([green_half] * lax.axis_size('loop')), 'loop', 0...  262 us
    reduce_scatter x1, waiting for transfers between devices, local(): lax.psum_scatter(full_bias, 'orb', scatter_dimension=0, tiled=True)  77.2 us
    gather x2, local copies, waits for them, and re-layouts, local(): full_bias = jnp.take(compact_bias, jnp.take(walker_index, anchor), axis=0)  11 us
    all_to_all x1, starting transfers between devices, local(): lax.all_to_all(jnp.stack([green_half] * lax.axis_size('loop')), 'loop', 0...  10.6 us
  transfers between devices with their start and end apart: 3, of which 2 were waited for; matrix products, arithmetic and copies ran while one was open for 8% of the time, Pallas kernels for 0%

profile of v1, /device:TPU:8, one launch (start us, length us, event | category | flops | bytes accessed | tf_op | source)
XLA Modules:
  0.0 406.5 jit_solution(10649620991639112360)
XLA Ops:
  8.0 1.1 copy.10
  9.1 6.1 %stack.2 = bf16[32,48,4096]{2,1,0:T(8,128)(2,1)} broadcast(bf16[48,4096]{1,0:T(8,128)(2,1)S(1)} %copy.10), dimensions={1,2} | broadcast | bytes 12976128 | tf_op jit(solution)/shard_map/stack | solution.py:39
  15.2 10.6 %all-to-all-start = ((bf16[32,48,4096]{2,1,0:T(8,128)(2,1)}), bf16[32,48,4096]{2,1,0:T(8,128)(2,1)}, u32[]{:S(2)}, u32[]{:S(2)}) async-start(bf16[32,48,4096]{2,1,0:T(8,128)(2,1)} %stack.2), calls=%async_computation | async-start | bytes 25165824 | tf_op jit(solution)/shard_map/all_to_all | solution.py:39
  25.9 0.3 reduce-window.27
  26.3 0.1 slice_reduce_fusion
  26.5 2.3 scatter_custom_fusion.1
  28.8 0.2 reduce-window.29
  29.0 0.6 fusion.8
  29.7 0.7 compare_select_fusion.6
  30.3 0.6 gather_fusion.5
  31.0 0.7 compare_and_fusion.2
  31.7 0.6 gather_fusion.1
  32.2 0.7 broadcast_select_fusion.1
  33.0 0.3 fusion
  33.3 0.7 fusion.17
  34.1 0.1 copy.7
  34.2 0.1 fusion.6
  34.4 0.9 scatter_custom_fusion
  35.3 0.2 select_n.234
  35.4 0.6 select_reduce_fusion
  36.1 8.4 %gather_fusion.2 = s32[1536]{0:T(1024)S(1)} fusion(s32[1536]{0:T(1024)S(1)} %iota.34, s32[2048]{0:T(1024)S(1)} %pad_clamp_fusion.1), kind=kCustom, calls=%fused_computation.5 | custom fusion | bytes 18432 | tf_op jit(solution)/shard_map/jit(_take)/gather | solution.py:61
  44.6 262.4 %all-to-all-done = bf16[32,48,4096]{2,1,0:T(8,128)(2,1)} async-done(((bf16[32,48,4096]{2,1,0:T(8,128)(2,1)}), bf16[32,48,4096]{2,1,0:T(8,128)(2,1)}, u32[]{:S(2)}, u32[]{:S(2)}) %all-to-all-start) | async-done | bytes 12582944 | tf_op jit(solution)/shard_map/all_to_all | solution.py:39
  307.0 6.4 %fusion.21 = f32[1536,128]{1,0:T(8,128)S(1)} fusion(bf16[1536,4096]{1,0:T(8,128)(2,1)} %bitcast.13, bf16[128,4096]{1,0:T(8,128)(2,1)S(1)} %copy-done), kind=kOutput, calls=%fused_computation.85 | convolution fusion | flops 1610612736 | bytes 14417920 | tf_op jit(solution)/shard_map/dot_general | solution.py:8
  313.4 2.6 gather_fusion.3
  316.0 1.1 broadcast_select_fusion
  317.2 0.6 fusion.11
  317.8 0.6 gather_fusion
  318.4 0.6 compare_select_fusion.7
  319.0 0.2 convert_reduce_fusion
  319.2 0.6 gather_fusion.4
  319.9 1.9 scatter_custom_fusion.2
  321.8 77.2 %reduce-scatter.2.cloned.1.call-done = f32[96,128]{1,0:T(8,128)} async-done(((f32[1536,128]{1,0:T(8,128)}), f32[96,128]{1,0:T(8,128)}) %reduce-scatter.2.cloned.1.call-update) | async-done | bytes 49168 | tf_op jit(solution)/shard_map/reduce_scatter | solution.py:62
  (36 shorter events, 0.7 us)
Async XLA Ops:
  8.0 299.0 %copy-start = (bf16[128,4096]{1,0:T(8,128)(2,1)S(1)}, bf16[128,4096]{1,0:T(8,128)(2,1)}, u32[]{:S(2)}) copy-start(bf16[128,4096]{1,0:T(8,128)(2,1)} %param.5) | copy-start | bytes 3145732
  15.2 10.7 %copy-start.2 = (s32[256,2]{0,1:T(2,128)S(1)}, s32[256,2]{0,1:T(2,128)}, u32[]{:S(2)}) copy-start(s32[256,2]{0,1:T(2,128)} %param.7) | copy-start | bytes 6148
  15.2 291.8 %all-to-all-start = ((bf16[32,48,4096]{2,1,0:T(8,128)(2,1)}), bf16[32,48,4096]{2,1,0:T(8,128)(2,1)}, u32[]{:S(2)}, u32[]{:S(2)}) async-start(bf16[32,48,4096]{2,1,0:T(8,128)(2,1)} %stack.2), calls=%async_computation | async-start | bytes 25165824 | tf_op jit(solution)/shard_map/all_to_all | solution.py:39
  25.8 294.1 %all-gather.2.cloned.1.call-start = ((), (), s32[]{:S(2)}) async-start(), calls=%async_computation.2 | async-start | bytes 2162688 | tf_op jit(solution)/shard_map/all_gather | solution.py:56
  33.0 366.0 %reduce-scatter.2.cloned.1.call-start = ((), (), s32[]{:S(2)}) async-start(), calls=%async_computation.3 | async-start | bytes 835584 | tf_op jit(solution)/shard_map/reduce_scatter | solution.py:62
  321.8 77.2 %copy-start.1 = (bf16[48,4096]{1,0:T(8,128)(2,1)}, bf16[48,4096]{1,0:T(8,128)(2,1)S(1)}, u32[]{:S(2)}) copy-start(bf16[48,4096]{1,0:T(8,128)(2,1)S(1)} %scatter_custom_fusion.2) | copy-start | bytes 1179652
Sparse Core Ops, SparseCore 0:
  33.1 118.0 all-gather.1
Sparse Core Ops, SparseCore 1:
  317.3 81.7 reduce-scatter.1
